TPU v7x, 128 devices: a whole 4x4x4 slice. The times are simulated.
128 devices in a mesh: view: 8 (over x, z_lo), seq: 16 (over y, z_hi, core).
Axes of the slice: x: 4, y: 4, z: 4 (z_hi: 2, z_lo: 2; z = z_hi * 2 + z_lo), core: 2. Of those that a mesh axis runs over, the one named last changes fastest.
Arguments:
- target: bfloat16 [8, 2048, 2048], P('view', 'seq'), may hold values from -6 to 6
- ref_slots: bfloat16 [8, 2048, 2048], P('view', 'seq'), may hold values from -6 to 6
- owners: int32 [4], replicated, may hold values from 0 to 7, as said below
- norm_gain: float32 [2048], replicated, may hold values from 0.1 to 1.9
- w_qkv: bfloat16 [2048, 3, 2048], P(None, None, 'seq'), may hold values from -0.125 to 0.125
- head_scale: float32 [16], P('seq'), may hold values from 1.5 to 40
- w_out: bfloat16 [2048, 2048], P('seq'), may hold values from -0.5 to 0.5
Outputs:
- output: bfloat16 [8, 2048, 2048], P('view', 'seq')
Inputs may be any that keep to these rules, and one draw needn't show every extreme that they name: `owners`: the 4 entries are distinct slots; slot 0 and slot 7 are always among them.
All inputs are finite; a program needn't handle non-finite values.
Results may differ from a plain program's by a relative error of at most 0.02.
The roundings to bfloat16 on the way count: a program that leaves them out, or rounds other values in their place, can miss the bound.
Values may be sent and summed in bfloat16 or wider, within the bound.
A program may use at most 128 MiB of HBM per device.

v0:
```python
import jax
import jax.numpy as jnp
from jax import lax
from jax.sharding import PartitionSpec as P

HD = 128
REFS = 4


def spread(value, axis, source):
    kept = jnp.where(lax.axis_index(axis) == source, value, 0).astype(value.dtype)
    return lax.psum(kept, axis)


def rms_norm(x, gain):
    xf = x.astype(jnp.float32)
    scaled = xf * lax.rsqrt(jnp.mean(xf * xf, axis=-1, keepdims=True) + 1e-06)
    return (scaled * gain).astype(jnp.bfloat16)


def local(target, ref_slots, owners, norm_gain, w_qkv, head_scale, w_out):
    width = target.shape[2]
    head_cols = w_qkv.shape[2]
    local_heads = head_cols // HD
    view_count = target.shape[0]
    normed = rms_norm(target, norm_gain)
    w_flat = w_qkv.reshape(width, -1)
    w_pair = w_qkv[:, 1:, :].reshape(width, -1)
    qkv = jnp.einsum(
        "vtd,de->vte",
        lax.all_gather(normed, "seq", axis=1, tiled=True),
        w_flat,
        preferred_element_type=jnp.float32,
    ).astype(jnp.bfloat16)
    full_len = qkv.shape[1]
    qkv = qkv.reshape(view_count, full_len, 3, local_heads, HD)
    slot_normed = rms_norm(ref_slots, norm_gain)
    slot_kv = jnp.einsum(
        "vtd,de->vte",
        lax.all_gather(slot_normed, "seq", axis=1, tiled=True),
        w_pair,
        preferred_element_type=jnp.float32,
    ).astype(jnp.bfloat16)
    ref_kv = jnp.concatenate(
        [spread(slot_kv, "view", owners[index]) for index in range(REFS)], axis=0
    )
    ref_kv = ref_kv.reshape(REFS * full_len, 2, local_heads, HD)
    factor = head_scale * HD ** (-0.5)
    block = min(512, full_len)
    keys = jnp.concatenate([qkv[0, :, 1], ref_kv[:, 0]], axis=0)
    values = jnp.concatenate([qkv[0, :, 2], ref_kv[:, 1]], axis=0)
    blocks = qkv[0, :, 0].reshape(full_len // block, block, local_heads, HD)

    def attend_block(query):
        scores = (
            jnp.einsum("qhe,khe->hqk", query, keys, preferred_element_type=jnp.float32)
            * factor[:, None, None]
        )
        top = jnp.max(scores, axis=-1, keepdims=True)
        expo = jnp.exp(scores - top)
        weights = (expo / jnp.sum(expo, axis=-1, keepdims=True)).astype(jnp.bfloat16)
        return jnp.einsum(
            "hqk,khe->qhe", weights, values, preferred_element_type=jnp.float32
        ).astype(jnp.bfloat16)

    result = lax.map(attend_block, blocks)
    outputs = [result.reshape(full_len, head_cols)]
    attended = jnp.stack(outputs, axis=0)
    summed = lax.psum_scatter(
        jnp.einsum("vte,ed->tvd", attended, w_out, preferred_element_type=jnp.float32).astype(
            jnp.bfloat16
        ),
        "seq",
        scatter_dimension=0,
        tiled=True,
    ).astype(jnp.float32)
    return jnp.transpose(summed, (1, 0, 2)).astype(jnp.bfloat16)


def solution(mesh):
    placed = (
        P("view", "seq", None),
        P("view", "seq", None),
        P(),
        P(),
        P(None, None, "seq"),
        P("seq"),
        P("seq", None),
    )
    return jax.shard_map(
        local, mesh=mesh, in_specs=placed, out_specs=P("view", "seq", None), check_vma=False
    )
```

profile of v0, /device:TPU:1, one launch (start us, length us, event | category | flops | bytes accessed | tf_op | source)
XLA Modules:
  0.0 546.0 jit_solution(2526833763792240753)
XLA Ops:
  6.5 1.3 fusion.27
  7.8 1.2 fusion.30
  9.1 2.5 fusion.32
  11.6 0.7 all-gather.3.cloned.1.call-update
  15.5 1.7 copy.13
  17.3 70.8 %all-gather.5.cloned.1.call-done = bf16[1,2048,2048]{2,1,0:T(8,128)(2,1)} async-done(((bf16[1,128,2048]{2,1,0:T(8,128)(2,1)}), bf16[1,2048,2048]{2,1,0:T(8,128)(2,1)}) %all-gather.5.cloned.1.call-update) | async-done | bytes 8388624 | tf_op jit(solution)/shard_map/all_gather | solution.py:40
  88.2 7.8 %select_bitcast_fusion.3 = (bf16[1,2048,256]{2,1,0:T(8,128)(2,1)}, bf16[1,2048,256]{2,1,0:T(8,128)(2,1)}, bf16[1,2048,256]{2,1,0:T(8,128)(2,1)}, bf16[1,2048,256]{2,1,0:T(8,128)(2,1)}) fusion(pred[]{:T(512)S(6)} %eq.12, pred[]{:T(512)S(6)} %eq.15, pred[]{:T(512)S(6)} %eq.14, pred[]{:T(512)S(6)} %eq.13, bf16[2048,256]{0,1:T(8,128)(2,1)S(1)} %bitcast.98, ...), kind=kOutput, calls=%fused_computation.39 | convolution fusion | flops 2150105088 | bytes 13631492 | tf_op jit(solution)/shard_map/vtd,de->vte/dot_general | solution.py:38
  96.8 64.3 %all-gather.3.cloned.1.call-done = bf16[1,2048,2048]{2,1,0:T(8,128)(2,1)} async-done(((bf16[1,128,2048]{2,1,0:T(8,128)(2,1)}), bf16[1,2048,2048]{2,1,0:T(8,128)(2,1)}) %all-gather.3.cloned.1.call-update) | async-done | bytes 8388624 | tf_op jit(solution)/shard_map/all_gather | solution.py:31
  161.0 6.8 %fusion.21 = bf16[2048,384]{0,1:T(8,128)(2,1)S(1)} fusion(bf16[2048,384]{0,1:T(8,128)(2,1)S(1)} %bitcast.92, bf16[1,2048,2048]{2,1,0:T(8,128)(2,1)} %all-gather.3.cloned.1.call-done), kind=kOutput, calls=%fused_computation.20 | convolution fusion | flops 3222011904 | bytes 11534336 | tf_op jit(solution)/shard_map/vtd,de->vte/dot_general | solution.py:29
  168.3 1.0 copy.22
  169.3 1.0 copy.21
  170.3 174.8 %all-reduce.3.cloned.1.call-done = (bf16[1,2048,256]{2,1,0:T(8,128)(2,1)}, bf16[1,2048,256]{2,1,0:T(8,128)(2,1)}, bf16[1,2048,256]{2,1,0:T(8,128)(2,1)}, bf16[1,2048,256]{2,1,0:T(8,128)(2,1)}) async-done(((bf16[1,2048,256]{2,1,0:T(8,128)(2,1)}, bf16[1,2048,256]{2,1,0:T(8,128)(2,1)}, bf16[1,2048,256]{2,1,0:T(8,128)(2,1)}, bf16[1,2048,256]{2,1,0:T(8,128)(2,1)}), (bf16[1,2048,256]{2,1,0:T(8,128)(2,1)}, ...) | async-done | bytes 4194320 | tf_op jit(solution)/shard_map/psum | solution.py:12
  345.1 3.7 pad_maximum_fusion
  348.8 7.0 %reshape.113 = bf16[8192,2,1,128]{3,1,0,2:T(2,128)(2,1)} reshape(bf16[4,2048,256]{2,1,0:T(8,128)(2,1)} %pad_maximum_fusion) | data formatting | bytes 8388608 | tf_op jit(solution)/shard_map/reshape | solution.py:47
  355.8 8.8 %fusion.33 = (bf16[8192,1,1,128]{3,1,0,2:T(2,128)(2,1)S(1)}, bf16[8192,1,1,128]{3,1,0,2:T(2,128)(2,1)S(1)}) fusion(bf16[8192,2,1,128]{3,1,0,2:T(2,128)(2,1)} %reshape.113), kind=kLoop, calls=%fused_computation.42 | loop fusion | bytes 8388608 | tf_op jit(solution)/shard_map/slice | solution.py:51
  365.2 4.8 pad_maximum_fusion.2
  369.9 3.7 pad_maximum_fusion.1
  373.6 55.4 %while.10 = (s32[]{:T(128)}, bf16[4,512,1,128]{3,1,2,0:T(8,128)(2,1)}, bf16[4,512,1,128]{3,1,2,0:T(8,128)(2,1)}, bf16[10240,1,128]{2,0,1:T(8,128)(2,1)S(1)}, f32...) while((s32[]{:T(128)}, bf16[4,512,1,128]{3,1,2,0:T(8,128)(2,1)}, ...), condition=%wide.region_9.10_spmd, body=%wide.region_6.9_spmd.sunk | while | flops 2731604992 | bytes 78917744 | solution.py:66
  373.6 3.9 multiply_reduce_fusion.2
  377.5 4.1 fusion.46
  381.6 5.9 %fusion.47 = bf16[4,512,1,128]{3,1,2,0:T(8,128)(2,1)} fusion(bf16[4,512,1,128]{3,1,2,0:T(8,128)(2,1)} %get-tuple-element.128, s32[]{:T(128)} %get-tuple-element.127, bf16[10240,1,128]{2,0,1:T(8,128)(2,1)S(1)} %copy-done.1, f32[512,10240]{1,0:T(8,128)S(1)} %get-tuple-element.118, f32[512]{0:T(512)S(1)} %fusion.46, f32[512]{0:T(512)S(1)} %get-tuple-element.119, ...), kind=kOutput, calls=%fused_computation.10.clone.1 | convolution fusion | flops 1363214336 | bytes 23729152 | tf_op jit(solution)/shard_map/while/body/eval_jaxpr/hqk,khe->qhe/dot_general | solution.py:62
  387.5 3.9 multiply_reduce_fusion.2
  391.4 4.1 fusion.46
  395.4 5.9 %fusion.47 = bf16[4,512,1,128]{3,1,2,0:T(8,128)(2,1)} fusion(bf16[4,512,1,128]{3,1,2,0:T(8,128)(2,1)} %get-tuple-element.128, s32[]{:T(128)} %get-tuple-element.127, bf16[10240,1,128]{2,0,1:T(8,128)(2,1)S(1)} %copy-done.1, f32[512,10240]{1,0:T(8,128)S(1)} %get-tuple-element.118, f32[512]{0:T(512)S(1)} %fusion.46, f32[512]{0:T(512)S(1)} %get-tuple-element.119, ...), kind=kOutput, calls=%fused_computation.10.clone.1 | convolution fusion | flops 1363214336 | bytes 23729152 | tf_op jit(solution)/shard_map/while/body/eval_jaxpr/hqk,khe->qhe/dot_general | solution.py:62
  401.3 3.9 multiply_reduce_fusion.2
  405.2 4.1 fusion.46
  409.3 5.9 %fusion.47 = bf16[4,512,1,128]{3,1,2,0:T(8,128)(2,1)} fusion(bf16[4,512,1,128]{3,1,2,0:T(8,128)(2,1)} %get-tuple-element.128, s32[]{:T(128)} %get-tuple-element.127, bf16[10240,1,128]{2,0,1:T(8,128)(2,1)S(1)} %copy-done.1, f32[512,10240]{1,0:T(8,128)S(1)} %get-tuple-element.118, f32[512]{0:T(512)S(1)} %fusion.46, f32[512]{0:T(512)S(1)} %get-tuple-element.119, ...), kind=kOutput, calls=%fused_computation.10.clone.1 | convolution fusion | flops 1363214336 | bytes 23729152 | tf_op jit(solution)/shard_map/while/body/eval_jaxpr/hqk,khe->qhe/dot_general | solution.py:62
  415.2 3.9 multiply_reduce_fusion.2
  419.1 4.1 fusion.46
  423.2 5.9 %fusion.47 = bf16[4,512,1,128]{3,1,2,0:T(8,128)(2,1)} fusion(bf16[4,512,1,128]{3,1,2,0:T(8,128)(2,1)} %get-tuple-element.128, s32[]{:T(128)} %get-tuple-element.127, bf16[10240,1,128]{2,0,1:T(8,128)(2,1)S(1)} %copy-done.1, f32[512,10240]{1,0:T(8,128)S(1)} %get-tuple-element.118, f32[512]{0:T(512)S(1)} %fusion.46, f32[512]{0:T(512)S(1)} %get-tuple-element.119, ...), kind=kOutput, calls=%fused_computation.10.clone.1 | convolution fusion | flops 1363214336 | bytes 23729152 | tf_op jit(solution)/shard_map/while/body/eval_jaxpr/hqk,khe->qhe/dot_general | solution.py:62
  429.0 6.6 %convert_bitcast_fusion = bf16[2048,1,2048]{2,0,1:T(8,128)(2,1)} fusion(bf16[2048,128]{1,0:T(8,128)(2,1)} %bitcast.97, bf16[128,2048]{1,0:T(8,128)(2,1)S(1)} %copy-done), kind=kOutput, calls=%fused_computation.18 | convolution fusion | flops 1077936128 | bytes 9437184 | tf_op jit(solution)/shard_map/vte,ed->tvd/dot_general | solution.py:70
  435.7 103.8 %reduce-scatter.2.cloned.1.call-done = bf16[128,1,2048]{2,0,1:T(8,128)(2,1)} async-done(((bf16[2048,1,2048]{2,0,1:T(8,128)(2,1)}), bf16[128,1,2048]{2,0,1:T(8,128)(2,1)}) %reduce-scatter.2.cloned.1.call-update) | async-done | bytes 524304 | tf_op jit(solution)/shard_map/reduce_scatter | solution.py:69
  (29 shorter events, 1.9 us)
Async XLA Ops:
  6.5 422.5 %copy-start = (bf16[128,2048]{1,0:T(8,128)(2,1)S(1)}, bf16[128,2048]{1,0:T(8,128)(2,1)}, u32[]{:S(2)}) copy-start(bf16[128,2048]{1,0:T(8,128)(2,1)} %param.15) | copy-start | bytes 1572868
  6.5 5.9 %copy-start.3 = (s32[4]{0:T(128)S(1)}, s32[4]{0:T(128)}, u32[]{:S(2)}) copy-start(s32[4]{0:T(128)} %param.11) | copy-start | bytes 52
  6.5 81.6 %all-gather.5.cloned.1.call-start = ((), (), s32[]{:S(2)}) async-start(), calls=%async_computation.2 | async-start | bytes 8912896 | tf_op jit(solution)/shard_map/all_gather | solution.py:40
  11.6 149.5 %all-gather.3.cloned.1.call-start = ((), (), s32[]{:S(2)}) async-start(), calls=%async_computation.1 | async-start | bytes 8912896 | tf_op jit(solution)/shard_map/all_gather | solution.py:31
  12.3 332.8 %all-reduce.3.cloned.1.call-start = ((), (), s32[]{:S(2)}) async-start(), calls=%async_computation.4 | async-start | bytes 8388608 | tf_op jit(solution)/shard_map/psum | solution.py:12
  96.0 443.4 %reduce-scatter.2.cloned.1.call-start = ((), (), s32[]{:S(2)}) async-start(), calls=%async_computation.3 | async-start | bytes 8912896 | tf_op jit(solution)/shard_map/reduce_scatter | solution.py:69
  365.2 4.8 copy-start.2
  377.5 4.1 copy-start.1
  391.4 4.1 copy-start.1
  405.2 4.1 copy-start.1
  419.1 4.1 copy-start.1
Sparse Core Ops, SparseCore 0:
  11.7 76.4 all-gather.4
  90.6 70.4 all-gather.2
  163.8 181.2 all-reduce.2
  435.8 103.6 reduce-scatter.1
where the time goes:
time: 547 us; the launch traced here: 546 us
  waiting for transfers between devices  415 us (76%)
  matrix products  60.3 us (11%)
  other arithmetic  33.4 us (6%)
  local copies, waits for them, and re-layouts  21.3 us (4%)
  between operations  16.3 us (3%)
    psum x1, waiting for transfers between devices, spread(): return lax.psum(kept, axis)  175 us
    reduce_scatter x1, waiting for transfers between devices, local(): lax.psum_scatter(jnp.einsum('vte,ed->tvd', attended, w_out, preferred_ele...  104 us
    all_gather x1, waiting for transfers between devices, local(): lax.all_gather(slot_normed, 'seq', axis=1, tiled=True)  70.8 us
    all_gather x1, waiting for transfers between devices, local(): lax.all_gather(normed, 'seq', axis=1, tiled=True)  64.3 us
    dot_general x4, matrix products, attend_block(): jnp.einsum('hqk,khe->qhe', weights, values, preferred_element_type=jnp.fl...  23.6 us
    reduce_sum x4, other arithmetic, attend_block(): jnp.sum(expo, axis=-1, keepdims=True)  16.3 us
    dot_general x4, matrix products, attend_block(): jnp.einsum('qhe,khe->hqk', query, keys, preferred_element_type=jnp.float32)  15.5 us
  transfers between devices with their start and end apart: 4, of which 4 were waited for; matrix products, arithmetic and copies ran while one was open for 4% of the time, Pallas kernels for 0%

commit v1 on v0

v1 whole, which is shorter than its diff:
```python
import math

import jax
import jax.numpy as jnp
from jax import lax
from jax.experimental import pallas as pl
from jax.experimental.pallas import tpu as pltpu
from jax.sharding import PartitionSpec as P

HD = 128
D = 2048
LEN = 2048
TB = 128
SB = 64
RC = 1024
QB = 512
MESH = pl.DeviceIdType.MESH
F32 = jnp.float32
BF16 = jnp.bfloat16
NT = (((1,), (1,)), ((), ()))


def rows(start, size):
    return pl.ds(pl.multiple_of(start, size), size)


def normalise(x, gain):
    xf = x.astype(F32)
    scaled = xf * lax.rsqrt(jnp.mean(xf * xf, axis=-1, keepdims=True) + 1e-06)
    return (scaled * gain).astype(BF16)


class Gather:
    def __init__(self, buf, size, place, me, ring, partner, sibling, send, recv):
        self.buf, self.size, self.place = buf, size, place
        self.pos, self.side = me
        self.ring, self.partner, self.sibling = ring, partner, sibling
        self.send, self.recv = send, recv
        self.started = []

    def region(self, shift, k, half=None):
        pos = lax.rem(self.pos + shift, 4)
        side = self.side if k == 0 else 1 - self.side
        start = self.place(pos, side) * self.size
        if half is None:
            return self.buf.at[rows(start, self.size)]
        part = self.size // 2
        return self.buf.at[rows(start + half * part, part)]

    def put(self, region, device, sem):
        copy = pltpu.make_async_remote_copy(
            src_ref=region,
            dst_ref=region,
            send_sem=self.send.at[len(self.started)],
            recv_sem=self.recv.at[sem],
            device_id=device,
            device_id_type=MESH,
        )
        copy.start()
        self.started.append(copy)

    def got(self, region, sem):
        pltpu.make_async_remote_copy(
            src_ref=region,
            dst_ref=region,
            send_sem=self.send.at[0],
            recv_sem=self.recv.at[sem],
            device_id=self.partner,
            device_id_type=MESH,
        ).wait_recv()

    def share(self, shift, k):
        if self.sibling is not None:
            self.put(self.region(shift, k), self.sibling, 9 + {0: 0, 3: 2, 1: 4, 2: 6}[shift] + k)

    def own(self):
        block = self.region(0, 0)
        self.put(block, self.partner, 0)
        self.put(block, self.ring[0], 1)
        self.put(block, self.ring[1], 3)
        self.share(0, 0)

    def wait_partner(self):
        self.got(self.region(0, 1), 0)

    def pass_partner(self):
        block = self.region(0, 1)
        self.put(block, self.ring[0], 2)
        self.put(block, self.ring[1], 4)
        self.share(0, 1)

    def on_below(self, k):
        self.got(self.region(3, k), 1 + k)
        self.put(self.region(3, k, 0), self.ring[0], 5 + k)
        self.share(3, k)

    def on_above(self, k):
        self.got(self.region(1, k), 3 + k)
        self.put(self.region(1, k, 1), self.ring[1], 7 + k)
        self.share(1, k)

    def on_far(self, k):
        self.got(self.region(2, k, 0), 5 + k)
        self.got(self.region(2, k, 1), 7 + k)
        self.share(2, k)

    def wait_shared(self, sibling_region):
        for index, shift in enumerate((0, 3, 1, 2)):
            for k in range(2):
                self.got(sibling_region(shift, k), 9 + 2 * index + k)

    def close(self):
        for copy in self.started:
            copy.wait_send()


def kernel(
    x_ref, slot_ref, gain_ref, w_ref, scale_ref, sel_ref, wout_ref, out_ref,
    tok, ref_tok, wo, kv, query, acc, top, att, att_in, keep, give, moved, arrived,
    t_send, t_recv, s_send, s_recv, w_send, w_recv, r_send, r_recv, a_send, a_recv,
    m_send, m_recv,
):
    view, seq = lax.axis_index("view"), lax.axis_index("seq")
    x, zl = view // 2, lax.rem(view, 2)
    y, zh, core = seq // 4, lax.rem(seq // 2, 2), lax.rem(seq, 2)

    def seq_of(y_, zh_, c_):
        return (y_ * 2 + zh_) * 2 + c_

    y_up, y_down = lax.rem(y + 1, 4), lax.rem(y + 3, 4)
    x_up, x_down = lax.rem(x + 1, 4), lax.rem(x + 3, 4)
    seq_ring = ((view, seq_of(y_up, zh, core)), (view, seq_of(y_down, zh, core)))
    seq_partner = (view, seq_of(y, 1 - zh, core))
    sibling = (view, seq_of(y, zh, 1 - core))
    view_ring = ((x_up * 2 + zl, seq), (x_down * 2 + zl, seq))
    view_partner = (x * 2 + 1 - zl, seq)

    peers = []
    for dy in range(4):
        for dz in range(2):
            for dc in range(2):
                if (dy, dz, dc) != (0, 0, 0):
                    zh_ = zh if dz == 0 else 1 - zh
                    c_ = core if dc == 0 else 1 - core
                    peers.append((view, seq_of(lax.rem(y + dy, 4), zh_, c_)))
    peers += [view_partner, view_ring[0], view_ring[1]]
    barrier = pltpu.get_barrier_semaphore()
    for peer in peers:
        pl.semaphore_signal(barrier, inc=1, device_id=peer, device_id_type=MESH)

    def seq_place(y_, zh_):
        return seq_of(y_, zh_, core)

    me = (y, zh)
    g_t = Gather(tok, TB, seq_place, me, seq_ring, seq_partner, sibling, t_send, t_recv)
    g_s = Gather(ref_tok, SB, seq_place, me, seq_ring, seq_partner, sibling, s_send, s_recv)
    g_w = Gather(wo, TB, seq_place, me, seq_ring, seq_partner, sibling, w_send, w_recv)
    g_r = Gather(
        kv, RC, lambda x_, zl_: x_ * 2 + zl_, (x, zl), view_ring, view_partner, None, r_send, r_recv
    )

    def of_sibling(buf, size):
        def region(shift, k):
            zh_ = zh if k == 0 else 1 - zh
            return buf.at[rows(seq_of(lax.rem(y + shift, 4), zh_, 1 - core) * size, size)]

        return region

    gain = gain_ref[...]
    keep[zl] = normalise(slot_ref[rows(zl * SB, SB), :], gain)
    give[...] = normalise(slot_ref[rows((1 - zl) * SB, SB), :], gain)
    pl.semaphore_wait(barrier, len(peers))
    swap = pltpu.make_async_remote_copy(
        src_ref=give, dst_ref=keep.at[zl], send_sem=m_send.at[0], recv_sem=m_recv.at[0],
        device_id=view_partner, device_id_type=MESH,
    )
    swap.start()
    tok[rows(seq * TB, TB), :] = normalise(x_ref[...], gain)
    g_t.own()
    wo[rows(seq * TB, TB), :] = wout_ref[...]

    pltpu.make_async_remote_copy(
        src_ref=give, dst_ref=keep.at[1 - zl], send_sem=m_send.at[0], recv_sem=m_recv.at[0],
        device_id=view_partner, device_id_type=MESH,
    ).wait_recv()
    even, odd = keep[0].astype(F32), keep[1].astype(F32)
    moved[...] = jnp.where(sel_ref[0:1, :] == 0.0, even, odd).astype(BF16)
    half = x // 2
    move = pltpu.make_async_remote_copy(
        src_ref=moved, dst_ref=arrived.at[half], send_sem=m_send.at[1], recv_sem=m_recv.at[1 + half],
        device_id=((x + 1 - 2 * half) * 2 + zl, seq), device_id_type=MESH,
    )
    move.start()
    mine = rows(seq * SB, SB)
    middle = jnp.logical_or(x == 1, x == 2)

    @pl.when(jnp.logical_not(middle))
    def _():
        ref_tok[mine, :] = jnp.where(
            sel_ref[1:2, :] == 0.0, keep[0].astype(F32), keep[1].astype(F32)
        ).astype(BF16)

    @pl.when(middle)
    def _():
        for side in range(2):
            pltpu.make_async_remote_copy(
                src_ref=moved, dst_ref=arrived.at[side], send_sem=m_send.at[1],
                recv_sem=m_recv.at[1 + side], device_id=view_partner, device_id_type=MESH,
            ).wait_recv()
        code = sel_ref[1:2, :]
        near = jnp.where(code == 0.0, keep[0].astype(F32), keep[1].astype(F32))
        far = jnp.where(code == 2.0, arrived[0].astype(F32), arrived[1].astype(F32))
        ref_tok[mine, :] = jnp.where(code < 1.5, near, far).astype(BF16)

    g_s.own()
    g_t.on_below(0)
    g_t.on_above(0)
    g_s.wait_partner()
    g_s.pass_partner()
    g_t.wait_partner()
    g_t.pass_partner()
    g_s.on_below(0)
    g_s.on_above(0)
    g_s.on_below(1)
    g_s.on_above(1)
    g_s.on_far(0)
    g_s.on_far(1)
    g_s.wait_shared(of_sibling(ref_tok, SB))

    def ref_project(i, _):
        own_kv = jnp.dot(ref_tok[rows(i * QB, QB), :], w_ref[:, HD:], preferred_element_type=F32)
        kv[rows(view * RC + i * QB, QB), :] = own_kv.astype(BF16)
        return 0

    lax.fori_loop(0, RC // QB, ref_project, 0)
    g_r.own()
    g_t.on_below(1)
    g_t.on_above(1)
    g_t.on_far(0)
    g_t.on_far(1)
    g_t.wait_shared(of_sibling(tok, TB))
    g_w.own()
    factor = scale_ref[...]

    def project(i, _):
        at = rows(i * QB, QB)
        qkv = jnp.dot(tok[at, :], w_ref[...], preferred_element_type=F32).astype(BF16)
        kv[rows(4 * LEN + i * QB, QB), :] = qkv[:, HD:]
        scaled = qkv[:, :HD].astype(F32) * factor
        high = scaled.astype(BF16)
        low = (scaled - high.astype(F32)).astype(BF16)
        query[at, :] = jnp.concatenate([high, low], axis=1)
        return 0

    lax.fori_loop(0, LEN // QB, project, 0)

    def attend(chunk, first, last):
        at = rows(chunk * LEN, LEN)
        keys, values = kv[at, :HD], kv[at, HD:]
        keys = jnp.concatenate([keys, keys], axis=1)
        values = jnp.concatenate([values, jnp.ones((LEN, HD), BF16)], axis=1)

        def block(t):
            return rows(lax.rem(y + 1 + t, 4) * QB, QB)

        def score(t):
            return lax.dot_general(query[block(t), :], keys, NT, preferred_element_type=F32)

        ahead = score(0)
        for t in range(LEN // QB):
            scores = ahead
            if t + 1 < LEN // QB:
                ahead = score(t + 1)
            q = block(t)
            peak = jnp.max(scores, axis=1, keepdims=True)
            if first:
                new = jnp.broadcast_to(peak, (QB, HD))
            else:
                old = top[q, :]
                new = jnp.maximum(old, peak)
            weights = jnp.exp2(scores - jnp.tile(new, (1, LEN // HD))).astype(BF16)
            total = jnp.dot(weights, values, preferred_element_type=F32)
            if not first:
                total += acc[q, :] * jnp.tile(jnp.exp2(old - new), (1, 2))
            if last:
                att[q, :] = (total[:, :HD] / total[:, HD:]).astype(BF16)
                last(t)
            else:
                top[q, :] = new
                acc[q, :] = total

    sent = []

    def hand_out(t):
        y_ = lax.rem(y + 1 + t, 4)
        for combo in range(4):
            zh_ = zh if combo < 2 else 1 - zh
            c_ = core if combo % 2 == 0 else 1 - core
            to = seq_of(y_, zh_, c_)
            if t == 3 and combo == 0:
                att_in[:, rows(seq * HD, HD)] = att[rows(seq * TB, TB), :]
                continue
            copy = pltpu.make_async_remote_copy(
                src_ref=att.at[rows(to * TB, TB)],
                dst_ref=att_in.at[:, rows(seq * HD, HD)],
                send_sem=a_send.at[t * 4 + combo],
                recv_sem=a_recv.at[t * 4 + combo],
                device_id=(view, to),
                device_id_type=MESH,
            )
            copy.start()
            sent.append(copy)

    g_r.wait_partner()
    g_r.pass_partner()
    attend(4, True, None)
    g_r.on_below(0)
    g_r.on_above(0)
    g_w.wait_partner()
    g_w.pass_partner()
    g_w.on_below(0)
    g_w.on_above(0)
    attend(x, False, None)
    g_r.on_below(1)
    g_r.on_above(1)
    attend(x_down, False, None)
    g_w.on_below(1)
    g_w.on_above(1)
    attend(x_up, False, None)
    g_w.on_far(0)
    g_w.on_far(1)
    g_r.on_far(0)
    g_r.on_far(1)
    attend(lax.rem(x + 2, 4), False, hand_out)

    g_w.wait_shared(of_sibling(wo, TB))
    for t in range(4):
        for combo in range(4):
            if t == 3 and combo == 0:
                continue
            y_ = lax.rem(y + 3 - t, 4)
            zh_ = zh if combo < 2 else 1 - zh
            c_ = core if combo % 2 == 0 else 1 - core
            pltpu.make_async_remote_copy(
                src_ref=att.at[rows(0, TB)],
                dst_ref=att_in.at[:, rows(seq_of(y_, zh_, c_) * HD, HD)],
                send_sem=a_send.at[0],
                recv_sem=a_recv.at[t * 4 + combo],
                device_id=sibling,
                device_id_type=MESH,
            ).wait_recv()

    def output(i, _):
        at = rows(i * QB, QB)
        out_ref[:, at] = jnp.dot(att_in[...], wo[:, at], preferred_element_type=F32).astype(BF16)
        return 0

    lax.fori_loop(0, D // QB, output, 0)
    swap.wait_send()
    move.wait_send()
    for gather in (g_t, g_s, g_w, g_r):
        gather.close()
    for copy in sent:
        copy.wait_send()


def local(target, ref_slots, owners, norm_gain, w_qkv, head_scale, w_out):
    x = lax.axis_index("view") // 2
    inner = jnp.logical_and(owners > 0, owners < 7)
    low = jnp.min(jnp.where(inner, owners, 99))
    high = jnp.max(jnp.where(inner, owners, -1))
    send = jnp.where(
        x == 0, 1, jnp.where(x == 1, jnp.where(high == 2, 0, 1), jnp.where(x == 2, jnp.where(low == 4, 0, 1), 0))
    )
    for_low = jnp.where(low == 1, 2, jnp.where(low == 2, 0, jnp.where(low == 3, 1, 3)))
    for_high = jnp.where(high == 6, 3, jnp.where(high == 4, 0, jnp.where(high == 5, 1, 2)))
    final = jnp.where(x == 0, 0, jnp.where(x == 1, for_low, jnp.where(x == 2, for_high, 1)))
    row = jnp.arange(8)[:, None]
    sel = jnp.broadcast_to(jnp.where(row == 0, send, final).astype(F32), (8, D))
    factor = jnp.broadcast_to((head_scale * (HD ** (-0.5) * math.log2(math.e)))[:, None], (1, HD))
    vmem = pl.BlockSpec(memory_space=pltpu.VMEM)
    dma = pltpu.SemaphoreType.DMA
    out = pl.pallas_call(
        kernel,
        out_shape=jax.ShapeDtypeStruct((TB, D), BF16),
        in_specs=[vmem] * 7,
        out_specs=vmem,
        scratch_shapes=[
            pltpu.VMEM((LEN, D), BF16),
            pltpu.VMEM((RC, D), BF16),
            pltpu.VMEM((D, D), BF16),
            pltpu.VMEM((5 * LEN, 2 * HD), BF16),
            pltpu.VMEM((LEN, 2 * HD), BF16),
            pltpu.VMEM((LEN, 2 * HD), F32),
            pltpu.VMEM((LEN, HD), F32),
            pltpu.VMEM((LEN, HD), BF16),
            pltpu.VMEM((TB, D), BF16),
            pltpu.VMEM((2, SB, D), BF16),
            pltpu.VMEM((SB, D), BF16),
            pltpu.VMEM((SB, D), BF16),
            pltpu.VMEM((2, SB, D), BF16),
            dma((17,)), dma((17,)), dma((17,)), dma((17,)), dma((17,)), dma((17,)),
            dma((9,)), dma((9,)), dma((16,)), dma((16,)), dma((2,)), dma((3,)),
        ],
        compiler_params=pltpu.CompilerParams(
            collective_id=0, has_side_effects=True, vmem_limit_bytes=60 * 2**20
        ),
        cost_estimate=pl.CostEstimate(
            flops=18_000_000_000, bytes_accessed=4_000_000, transcendentals=21_000_000
        ),
    )(
        target[0], ref_slots[0], norm_gain[None, :], w_qkv.reshape(D, 3 * HD), factor, sel, w_out
    )
    return out[None]


def solution(mesh):
    placed = (
        P("view", "seq", None),
        P("view", "seq", None),
        P(),
        P(),
        P(None, None, "seq"),
        P("seq"),
        P("seq", None),
    )
    return jax.shard_map(
        local, mesh=mesh, in_specs=placed, out_specs=P("view", "seq", None), check_vma=False
    )
```

time: 547 us -> 141 us (0.26)
  waiting for transfers between devices: 415 us -> 0 us
  Pallas kernels: 0 us -> 128 us
  matrix products: 60.3 us -> 0 us
  other arithmetic: 33.4 us -> 0.67 us
  local copies, waits for them, and re-layouts: 21.3 us -> 6.42 us
  between operations: 16.3 us -> 5.75 us
    psum x1 -> x0, waiting for transfers between devices: 175 us -> none  [spread(): return lax.psum(kept, axis)]
    all_gather x2 -> x0, waiting for transfers between devices: 135 us -> none  [the longest x1 70.8 us: local(): lax.all_gather(slot_normed, 'seq', axis=1, tiled=True)]
    pallas_call x0 -> x1, Pallas kernels: none -> 128 us  [local(): pl.pallas_call(kernel, out_shape=jax.ShapeDtypeStruct((TB, D), BF16), in_...]
    reduce_scatter x1 -> x0, waiting for transfers between devices: 104 us -> none  [local(): lax.psum_scatter(jnp.einsum('vte,ed->tvd', attended, w_out, preferred_ele...]
    dot_general x11 -> x0, matrix products: 60.3 us -> none  [the longest x4 23.6 us: attend_block(): jnp.einsum('hqk,khe->qhe', weights, values, preferred_element_type=jnp.fl...]
    reduce_sum x6 -> x0, other arithmetic: 18.8 us -> none  [the longest x4 16.3 us: attend_block(): jnp.sum(expo, axis=-1, keepdims=True)]
    concatenate x3 -> x0, other arithmetic: 12.1 us -> none  [the longest x1 4.75 us: local(): values = jnp.concatenate([qkv[0, :, 2], ref_kv[:, 1]], axis=0)]
    slice x4 -> x0, local copies, waits for them, and re-layouts: 9.67 us -> none  [the longest x2 8.92 us: local(): values = jnp.concatenate([qkv[0, :, 2], ref_kv[:, 1]], axis=0)]
  transfers between devices with their start and end apart: 4 -> 0, of which waited for: 4 -> 0; matrix products, arithmetic and copies ran while one was open for 4% -> 0% of each run, Pallas kernels for 0% -> 0%
where the time goes in v1:
time: 141 us; the launch traced here: 140 us
  Pallas kernels  128 us (91%)
  local copies, waits for them, and re-layouts  6.42 us (5%)
  between operations  5.75 us (4%)
    pallas_call x1, Pallas kernels, local(): pl.pallas_call(kernel, out_shape=jax.ShapeDtypeStruct((TB, D), BF16), in_...  128 us
    unnamed x4, local copies, waits for them, and re-layouts  3.61 us

profile of v1, /device:TPU:1, one launch (start us, length us, event | category | flops | bytes accessed | tf_op | source)
XLA Modules:
  0.0 140.5 jit_solution(17295570243071234358)
XLA Ops:
  0.0 1.7 %copy.9 = bf16[2048,3,128]{0,2,1:T(8,128)(2,1)S(1)} copy(bf16[2048,3,128]{2,0,1:T(8,128)(2,1)} %param.11) | data formatting | bytes 3145728 | tf_op args[4]
  1.7 0.0 copy-start
  1.7 1.6 %copy.10.w_ref = bf16[2048,384]{1,0:T(8,128)(2,1)} copy(bf16[2048,384]{0,1:T(8,128)(2,1)S(1)} %bitcast.6) | data formatting | bytes 3145728 | tf_op jit(solution)/shard_map/reshape | solution.py:412
  4.0 0.5 broadcast_in_dim.37.scale_ref
  4.5 0.0 copy-done
  4.5 0.7 fusion.2
  10.2 0.7 broadcast_in_dim.42.sel_ref
  10.9 127.6 %shard_map.73 = bf16[128,2048]{1,0:T(8,128)(2,1)} custom-call(bf16[128,2048]{1,0:T(8,128)(2,1)} %bitcast.8, bf16[128,2048]{1,0:T(8,128)(2,1)} %bitcast.9, f32[1,2048]{1,0:T(1,128)} %bitcast.10, bf16[2048,384]{1,0:T(8,128)(2,1)} %copy.10.w_ref, f32[1,128]{1,0:T(1,128)} %broadcast_in_dim.37.scale_ref, f32[8,2048]{1,0:T(8,128)} %broadcast_in_dim.42.sel_ref, ...), custom_call_target="tpu_custom_call" | custom-call | flops 17999998976 | bytes 4000000 | tf_op jit(solution)/shard_map/pallas_call | solution.py:383
  138.6 1.9 %copy.13 = bf16[1,128,2048]{2,1,0:T(8,128)(2,1)} copy(bf16[1,128,2048]{2,1,0:T(8,128)(2,1)} %bitcast.7) | data formatting | bytes 1048576
  (1 shorter events, 0.0 us)
Async XLA Ops:
  1.7 2.8 %copy-start = (s32[4]{0:T(128)S(1)}, s32[4]{0:T(128)}, u32[]{:S(2)}) copy-start(s32[4]{0:T(128)} %param.9) | copy-start | bytes 52

commit v2 on v1

v2 whole, which is shorter than its diff:
```python
import math

import jax
import jax.numpy as jnp
from jax import lax
from jax.experimental import pallas as pl
from jax.experimental.pallas import tpu as pltpu
from jax.sharding import PartitionSpec as P

HD = 128
D = 2048
LEN = 2048
TB = 128
SB = 64
RC = 1024
QB = 512
MESH = pl.DeviceIdType.MESH
F32 = jnp.float32
BF16 = jnp.bfloat16
NT = (((1,), (1,)), ((), ()))


def rows(start, size):
    return pl.ds(pl.multiple_of(start, size), size)


def normalise(x, gain):
    xf = x.astype(F32)
    scaled = xf * lax.rsqrt(jnp.mean(xf * xf, axis=-1, keepdims=True) + 1e-06)
    return (scaled * gain).astype(BF16)


class Copies:
    def __init__(self, buf, size, place, me, ring, partner, sibling, send, recv):
        self.buf, self.size, self.place = buf, size, place
        self.pos, self.side = me
        self.ring, self.partner, self.sibling = ring, partner, sibling
        self.send, self.recv = send, recv
        self.started = []

    def region(self, shift, k, half=None):
        pos = lax.rem(self.pos + shift, 4)
        side = self.side if k == 0 else 1 - self.side
        start = self.place(pos, side) * self.size
        if half is None:
            return self.buf.at[rows(start, self.size)]
        part = self.size // 2
        return self.buf.at[rows(start + half * part, part)]

    def put(self, region, device, sem):
        copy = pltpu.make_async_remote_copy(
            src_ref=region,
            dst_ref=region,
            send_sem=self.send.at[len(self.started)],
            recv_sem=self.recv.at[sem],
            device_id=device,
            device_id_type=MESH,
        )
        copy.start()
        self.started.append(copy)

    def got(self, region, sem):
        pltpu.make_async_remote_copy(
            src_ref=region,
            dst_ref=region,
            send_sem=self.send.at[0],
            recv_sem=self.recv.at[sem],
            device_id=self.partner,
            device_id_type=MESH,
        ).wait_recv()

    def close(self):
        for copy in self.started:
            copy.wait_send()


class PartnerFirst(Copies):
    def share(self, shift, k):
        self.put(self.region(shift, k), self.sibling, 9 + {0: 0, 3: 2, 1: 4, 2: 6}[shift] + k)

    def own(self):
        block = self.region(0, 0)
        self.put(block, self.partner, 0)
        self.put(block, self.ring[0], 1)
        self.put(block, self.ring[1], 3)
        self.share(0, 0)

    def pass_partner(self):
        block = self.region(0, 1)
        self.got(block, 0)
        self.put(block, self.ring[0], 2)
        self.put(block, self.ring[1], 4)
        self.share(0, 1)

    def on_below(self, k):
        self.got(self.region(3, k), 1 + k)
        self.put(self.region(3, k, 0), self.ring[0], 5 + k)
        self.share(3, k)

    def on_above(self, k):
        self.got(self.region(1, k), 3 + k)
        self.put(self.region(1, k, 1), self.ring[1], 7 + k)
        self.share(1, k)

    def on_far(self, k):
        self.got(self.region(2, k, 0), 5 + k)
        self.got(self.region(2, k, 1), 7 + k)
        self.share(2, k)

    def wait_shared(self, sibling_region, shift):
        for k in range(2):
            self.got(sibling_region(shift, k), 9 + {0: 0, 3: 2, 1: 4, 2: 6}[shift] + k)


class RingFirst(Copies):
    def share(self, shift, k):
        self.put(self.region(shift, k), self.sibling, 8 + shift * 2 + k)

    def own(self):
        block = self.region(0, 0)
        self.put(block, self.ring[0], 0)
        self.put(block, self.ring[1], 1)
        self.put(block, self.partner, 4)
        self.share(0, 0)

    def on_below(self):
        self.got(self.region(3, 0), 0)
        self.put(self.region(3, 0, 0), self.ring[0], 2)
        self.put(self.region(3, 0), self.partner, 7)
        self.share(3, 0)

    def on_above(self):
        self.got(self.region(1, 0), 1)
        self.put(self.region(1, 0, 1), self.ring[1], 3)
        self.put(self.region(1, 0), self.partner, 5)
        self.share(1, 0)

    def on_far(self):
        self.got(self.region(2, 0, 0), 2)
        self.got(self.region(2, 0, 1), 3)
        self.put(self.region(2, 0), self.partner, 6)
        self.share(2, 0)

    def on_partner(self, shift):
        self.got(self.region(shift, 1), 4 + shift)
        self.share(shift, 1)

    def wait_shared(self, sibling_region):
        for shift in range(4):
            for k in range(2):
                self.got(sibling_region(shift, k), 8 + shift * 2 + k)


class Views(Copies):
    def own(self):
        block = self.region(0, 0)
        self.put(block, self.partner, 0)
        self.put(block, self.ring[0], 1)
        self.put(block, self.ring[1], 2)

    def on_below(self):
        self.got(self.region(3, 0), 1)
        self.put(self.region(3, 0, 0), self.ring[0], 5)

    def on_above(self):
        self.got(self.region(1, 0), 2)
        self.put(self.region(1, 0, 1), self.ring[1], 6)

    def pass_partner(self):
        block = self.region(0, 1)
        self.got(block, 0)
        self.put(block, self.ring[0], 3)
        self.put(block, self.ring[1], 4)

    def on_far(self):
        self.got(self.region(2, 0, 0), 5)
        self.got(self.region(2, 0, 1), 6)
        self.put(self.region(2, 0), self.partner, 7)

    def last_below(self):
        self.got(self.region(3, 1), 3)

    def last_above(self):
        self.got(self.region(1, 1), 4)

    def last_far(self):
        self.got(self.region(2, 1), 7)


def kernel(
    owner_ref, scale_ref, x_hbm, slot_hbm, gain_ref, w_hbm, wout_hbm, out_ref,
    x_ref, slot_ref, w_ref, tok, ref_tok, wo, kv, query, acc, top, att, att_in, keep, give, moved, arrived,
    t_send, t_recv, s_send, s_recv, w_send, w_recv, r_send, r_recv, a_send, a_recv,
    m_send, m_recv, i_sem,
):
    view, seq = lax.axis_index("view"), lax.axis_index("seq")
    x, zl = view // 2, lax.rem(view, 2)
    y, zh, core = seq // 4, lax.rem(seq // 2, 2), lax.rem(seq, 2)

    def seq_of(y_, zh_, c_):
        return (y_ * 2 + zh_) * 2 + c_

    y_up, y_down = lax.rem(y + 1, 4), lax.rem(y + 3, 4)
    x_up, x_down = lax.rem(x + 1, 4), lax.rem(x + 3, 4)
    y_far, x_far = lax.rem(y + 2, 4), lax.rem(x + 2, 4)
    seq_ring = ((view, seq_of(y_up, zh, core)), (view, seq_of(y_down, zh, core)))
    seq_partner = (view, seq_of(y, 1 - zh, core))
    sibling = (view, seq_of(y, zh, 1 - core))
    view_ring = ((x_up * 2 + zl, seq), (x_down * 2 + zl, seq))
    view_partner = (x * 2 + 1 - zl, seq)
    cross = (x * 2 + 1 - zl, seq_of(y, 1 - zh, core))

    peers = []
    for dy in range(4):
        for dz in range(2):
            for dc in range(2):
                if (dy, dz, dc) != (0, 0, 0):
                    zh_ = zh if dz == 0 else 1 - zh
                    c_ = core if dc == 0 else 1 - core
                    peers.append((view, seq_of(lax.rem(y + dy, 4), zh_, c_)))
    peers += [view_partner, view_ring[0], view_ring[1], cross]
    barrier = pltpu.get_barrier_semaphore()
    for peer in peers:
        pl.semaphore_signal(barrier, inc=1, device_id=peer, device_id_type=MESH)

    load_slot = pltpu.make_async_copy(slot_hbm, slot_ref, i_sem.at[0])
    load_x = pltpu.make_async_copy(x_hbm, x_ref, i_sem.at[1])
    load_wo = pltpu.make_async_copy(wout_hbm, wo.at[rows(seq * TB, TB)], i_sem.at[2])
    load_w = [
        pltpu.make_async_copy(w_hbm.at[j], w_ref.at[:, j * HD : (j + 1) * HD], i_sem.at[3 + j])
        for j in range(3)
    ]
    for copy in [load_slot, load_x] + load_w + [load_wo]:
        copy.start()

    def seq_place(y_, zh_):
        return seq_of(y_, zh_, core)

    me = (y, zh)
    g_t = PartnerFirst(tok, TB, seq_place, me, seq_ring, seq_partner, sibling, t_send, t_recv)
    g_s = RingFirst(ref_tok, SB, seq_place, me, seq_ring, seq_partner, sibling, s_send, s_recv)
    g_w = PartnerFirst(wo, TB, seq_place, me, seq_ring, cross, sibling, w_send, w_recv)
    g_r = Views(
        kv, RC, lambda x_, zl_: x_ * 2 + zl_, (x, zl), view_ring, view_partner, None, r_send, r_recv
    )

    def of_sibling(buf, size):
        def region(shift, k):
            zh_ = zh if k == 0 else 1 - zh
            return buf.at[rows(seq_of(lax.rem(y + shift, 4), zh_, 1 - core) * size, size)]

        return region

    slots = [owner_ref[i] for i in range(4)]
    low, high = jnp.int32(99), jnp.int32(-1)
    for slot in slots:
        inner = jnp.logical_and(slot > 0, slot < 7)
        low = jnp.minimum(low, jnp.where(inner, slot, 99))
        high = jnp.maximum(high, jnp.where(inner, slot, -1))
    give_even = jnp.where(
        x == 0, 0, jnp.where(x == 1, (high == 2).astype(jnp.int32), jnp.where(x == 2, (low == 4).astype(jnp.int32), 1))
    )
    for_low = jnp.where(low == 1, 2, jnp.where(low == 2, 0, jnp.where(low == 3, 1, 3)))
    for_high = jnp.where(high == 6, 3, jnp.where(high == 4, 0, jnp.where(high == 5, 1, 2)))
    final = jnp.where(x == 0, 0, jnp.where(x == 1, for_low, jnp.where(x == 2, for_high, 1)))

    gain = gain_ref[...]
    load_slot.wait()
    give[...] = normalise(slot_ref[rows((1 - zl) * SB, SB), :], gain)
    pl.semaphore_wait(barrier, len(peers))
    part = SB // 2
    parts = [rows(i * part, part) for i in range(2)]

    def swap(i, side):
        return pltpu.make_async_remote_copy(
            src_ref=give.at[parts[i]], dst_ref=keep.at[side, parts[i]],
            send_sem=m_send.at[i], recv_sem=m_recv.at[i],
            device_id=view_partner, device_id_type=MESH,
        )

    half = x // 2

    def move(i, side):
        return pltpu.make_async_remote_copy(
            src_ref=moved.at[parts[i]], dst_ref=arrived.at[side, parts[i]],
            send_sem=m_send.at[2 + i], recv_sem=m_recv.at[2 + 2 * side + i],
            device_id=((x + 1 - 2 * half) * 2 + zl, seq), device_id_type=MESH,
        )

    for i in range(2):
        swap(i, zl).start()
    load_x.wait()
    tok[rows(seq * TB, TB), :] = normalise(x_ref[...], gain)
    g_t.own()
    keep[zl] = normalise(slot_ref[rows(zl * SB, SB), :], gain)
    for i in range(2):
        swap(i, 1 - zl).wait_recv()
        moved[parts[i], :] = jnp.where(
            give_even == 1, keep[0, parts[i], :].astype(F32), keep[1, parts[i], :].astype(F32)
        ).astype(BF16)
        move(i, half).start()
    mine = rows(seq * SB, SB)
    middle = jnp.logical_or(x == 1, x == 2)

    @pl.when(jnp.logical_not(middle))
    def _():
        ref_tok[mine, :] = jnp.where(final == 0, keep[0].astype(F32), keep[1].astype(F32)).astype(BF16)

    @pl.when(middle)
    def _():
        for i in range(2):
            for side in range(2):
                move(i, side).wait_recv()
        near = jnp.where(final == 0, keep[0].astype(F32), keep[1].astype(F32))
        far = jnp.where(final == 2, arrived[0].astype(F32), arrived[1].astype(F32))
        ref_tok[mine, :] = jnp.where(final < 2, near, far).astype(BF16)

    factor = scale_ref[0] * (HD ** (-0.5) * math.log2(math.e))

    def project(y_):
        at = rows(y_ * QB, QB)
        qkv = jnp.dot(tok[at, :], w_ref[...], preferred_element_type=F32).astype(BF16)
        kv[rows(4 * LEN + y_ * QB, QB), :] = qkv[:, HD:]
        scaled = qkv[:, :HD].astype(F32) * factor
        high_part = scaled.astype(BF16)
        low_part = (scaled - high_part.astype(F32)).astype(BF16)
        query[at, :] = jnp.concatenate([high_part, low_part], axis=1)

    tok_shared = of_sibling(tok, TB)
    g_s.own()
    g_t.pass_partner()
    g_t.on_below(0)
    g_t.on_above(0)
    for copy in load_w:
        copy.wait()
    g_s.on_below()
    g_s.on_above()
    g_s.on_partner(0)
    g_t.wait_shared(tok_shared, 0)
    project(y)
    g_t.on_below(1)
    g_t.on_above(1)
    g_s.on_far()
    g_s.on_partner(1)
    g_s.on_partner(3)
    g_s.on_partner(2)
    g_s.wait_shared(of_sibling(ref_tok, SB))

    def ref_project(i, _):
        own_kv = jnp.dot(ref_tok[rows(i * QB, QB), :], w_ref[:, HD:], preferred_element_type=F32)
        kv[rows(view * RC + i * QB, QB), :] = own_kv.astype(BF16)
        return 0

    lax.fori_loop(0, RC // QB, ref_project, 0)
    g_r.own()
    g_t.wait_shared(tok_shared, 3)
    project(y_down)
    g_t.wait_shared(tok_shared, 1)
    project(y_up)
    g_t.on_far(0)
    g_t.on_far(1)
    load_wo.wait()
    g_w.own()
    g_t.wait_shared(tok_shared, 2)
    project(y_far)

    def attend(starts, size, first=False, last=None):
        count = size * len(starts)
        pieces = [kv[rows(start, size), :] for start in starts]
        both = pieces[0] if len(pieces) == 1 else jnp.concatenate(pieces, axis=0)
        keys = jnp.concatenate([both[:, :HD], both[:, :HD]], axis=1)
        values = jnp.concatenate([both[:, HD:], jnp.ones((count, HD), BF16)], axis=1)

        def block(t):
            return rows(lax.rem(y + 1 + t, 4) * QB, QB)

        def score(t):
            return lax.dot_general(query[block(t), :], keys, NT, preferred_element_type=F32)

        ahead = score(0)
        for t in range(LEN // QB):
            scores = ahead
            if t + 1 < LEN // QB:
                ahead = score(t + 1)
            q = block(t)
            peak = jnp.max(scores, axis=1, keepdims=True)
            if first:
                new = jnp.broadcast_to(peak, (QB, HD))
            else:
                old = top[q, :]
                new = jnp.maximum(old, peak)
            weights = jnp.exp2(scores - jnp.tile(new, (1, count // HD))).astype(BF16)
            total = jnp.dot(weights, values, preferred_element_type=F32)
            if not first:
                total += acc[q, :] * jnp.tile(jnp.exp2(old - new), (1, 2))
            if last:
                att[q, :] = (total[:, :HD] / total[:, HD:]).astype(BF16)
                last(t)
            else:
                top[q, :] = new
                acc[q, :] = total

    sent = []

    def hand_out(t):
        y_ = lax.rem(y + 1 + t, 4)
        for combo in range(4):
            zh_ = zh if combo < 2 else 1 - zh
            c_ = core if combo % 2 == 0 else 1 - core
            to = seq_of(y_, zh_, c_)
            if t == 3 and combo == 0:
                att_in[:, rows(seq * HD, HD)] = att[rows(seq * TB, TB), :]
                continue
            copy = pltpu.make_async_remote_copy(
                src_ref=att.at[rows(to * TB, TB)],
                dst_ref=att_in.at[:, rows(seq * HD, HD)],
                send_sem=a_send.at[t * 4 + combo],
                recv_sem=a_recv.at[t * 4 + combo],
                device_id=(view, to),
                device_id_type=MESH,
            )
            copy.start()
            sent.append(copy)

    def group(x_, zl_):
        return (x_ * 2 + zl_) * RC

    attend([4 * LEN], LEN, first=True)
    g_r.on_below()
    g_r.on_above()
    g_r.pass_partner()
    g_w.pass_partner()
    attend([group(x, zl)], RC)
    g_w.on_below(0)
    g_w.on_above(0)
    attend([group(x, 1 - zl)], RC)
    g_r.on_far()
    attend([group(x_down, zl)], RC)
    attend([group(x_up, zl)], RC)
    g_w.on_below(1)
    g_w.on_above(1)
    attend([group(x_far, zl)], RC)
    g_r.last_below()
    attend([group(x_down, 1 - zl)], RC)
    g_w.on_far(0)
    g_w.on_far(1)
    g_r.last_above()
    g_r.last_far()
    attend([group(x_up, 1 - zl), group(x_far, 1 - zl)], RC, last=hand_out)

    for shift in range(4):
        g_w.wait_shared(of_sibling(wo, TB), shift)
    for t in range(4):
        for combo in range(4):
            if t == 3 and combo == 0:
                continue
            y_ = lax.rem(y + 3 - t, 4)
            zh_ = zh if combo < 2 else 1 - zh
            c_ = core if combo % 2 == 0 else 1 - core
            pltpu.make_async_remote_copy(
                src_ref=att.at[rows(0, TB)],
                dst_ref=att_in.at[:, rows(seq_of(y_, zh_, c_) * HD, HD)],
                send_sem=a_send.at[0],
                recv_sem=a_recv.at[t * 4 + combo],
                device_id=sibling,
                device_id_type=MESH,
            ).wait_recv()

    def output(i, _):
        at = rows(i * QB, QB)
        out_ref[:, at] = jnp.dot(att_in[...], wo[:, at], preferred_element_type=F32).astype(BF16)
        return 0

    lax.fori_loop(0, D // QB, output, 0)
    for i in range(2):
        swap(i, zl).wait_send()
        move(i, half).wait_send()
    for gather in (g_t, g_s, g_w, g_r):
        gather.close()
    for copy in sent:
        copy.wait_send()


def local(target, ref_slots, owners, norm_gain, w_qkv, head_scale, w_out):
    vmem = pl.BlockSpec(memory_space=pltpu.VMEM)
    smem = pl.BlockSpec(memory_space=pltpu.SMEM)
    hbm = pl.BlockSpec(memory_space=pl.ANY)
    dma = pltpu.SemaphoreType.DMA
    out = pl.pallas_call(
        kernel,
        out_shape=jax.ShapeDtypeStruct((TB, D), BF16),
        in_specs=[smem, smem, hbm, hbm, vmem, hbm, hbm],
        out_specs=vmem,
        scratch_shapes=[
            pltpu.VMEM((TB, D), BF16),
            pltpu.VMEM((TB, D), BF16),
            pltpu.VMEM((D, 3 * HD), BF16),
            pltpu.VMEM((LEN, D), BF16),
            pltpu.VMEM((RC, D), BF16),
            pltpu.VMEM((D, D), BF16),
            pltpu.VMEM((5 * LEN, 2 * HD), BF16),
            pltpu.VMEM((LEN, 2 * HD), BF16),
            pltpu.VMEM((LEN, 2 * HD), F32),
            pltpu.VMEM((LEN, HD), F32),
            pltpu.VMEM((LEN, HD), BF16),
            pltpu.VMEM((TB, D), BF16),
            pltpu.VMEM((2, SB, D), BF16),
            pltpu.VMEM((SB, D), BF16),
            pltpu.VMEM((SB, D), BF16),
            pltpu.VMEM((2, SB, D), BF16),
            dma((17,)), dma((17,)), dma((16,)), dma((16,)), dma((17,)), dma((17,)),
            dma((8,)), dma((8,)), dma((16,)), dma((16,)), dma((4,)), dma((6,)), dma((6,)),
        ],
        compiler_params=pltpu.CompilerParams(
            collective_id=0, has_side_effects=True, vmem_limit_bytes=60 * 2**20
        ),
        cost_estimate=pl.CostEstimate(
            flops=18_000_000_000, bytes_accessed=4_000_000, transcendentals=21_000_000
        ),
    )(
        owners, head_scale, target[0], ref_slots[0], norm_gain[None, :],
        jnp.transpose(w_qkv, (1, 0, 2)), w_out,
    )
    return out[None]


def solution(mesh):
    placed = (
        P("view", "seq", None),
        P("view", "seq", None),
        P(),
        P(),
        P(None, None, "seq"),
        P("seq"),
        P("seq", None),
    )
    return jax.shard_map(
        local, mesh=mesh, in_specs=placed, out_specs=P("view", "seq", None), check_vma=False
    )
```

time: 141 us -> 120 us (0.85)
  Pallas kernels: 128 us -> 118 us
  between operations: 5.75 us -> 0.66 us
  local copies, waits for them, and re-layouts: 6.42 us -> 1.88 us
    pallas_call x1, Pallas kernels: 128 us -> 118 us  [local(): pl.pallas_call(kernel, out_shape=jax.ShapeDtypeStruct((TB, D), BF16), in_...]
    unnamed x4 -> x1, local copies, waits for them, and re-layouts: 3.61 us -> 1.88 us
    reshape x1 -> x0, local copies, waits for them, and re-layouts: 1.6 us -> none  [local(): w_qkv.reshape(D, 3 * HD)]
where the time goes in v2:
time: 120 us
  Pallas kernels  118 us (98%)
  local copies, waits for them, and re-layouts  1.88 us (2%)
    pallas_call x1, Pallas kernels, local(): pl.pallas_call(kernel, out_shape=jax.ShapeDtypeStruct((TB, D), BF16), in_...  118 us

profile of v2, /device:TPU:1, one launch (start us, length us, event | category | flops | bytes accessed | tf_op | source)
XLA Modules:
  0.0 120.2 jit_solution(14784011324469402868)
XLA Ops:
  0.7 117.6 %shard_map.73 = bf16[128,2048]{1,0:T(8,128)(2,1)} custom-call(s32[4]{0:T(128)} %owner_ref.1, f32[1]{0:T(128)S(6)} %copy.9.scale_ref, bf16[128,2048]{1,0:T(8,128)(2,1)} %bitcast.7, bf16[128,2048]{1,0:T(8,128)(2,1)} %bitcast.8, f32[1,2048]{1,0:T(1,128)} %bitcast.9, bf16[3,2048,128]{2,1,0:T(8,128)(2,1)} %bitcast.6, bf16[128,2048]{1,0:T(8,128)(2,1)} %wout_hbm.1), custom_call_target="tpu_custom_call" | custom-call | flops 17999998976 | bytes 4000000 | tf_op jit(solution)/shard_map/pallas_call | solution.py:489
  118.3 1.9 %copy.10 = bf16[1,128,2048]{2,1,0:T(8,128)(2,1)} copy(bf16[1,128,2048]{2,1,0:T(8,128)(2,1)} %bitcast.5) | data formatting | bytes 1048576

commit v3 on v2

--- a/solution.py
+++ b/solution.py
@@ -41,7 +41,7 @@
     def region(self, shift, k, half=None):
         pos = lax.rem(self.pos + shift, 4)
         side = self.side if k == 0 else 1 - self.side
-        start = self.place(pos, side) * self.size
+        start = self.place(pos, side)
         if half is None:
             return self.buf.at[rows(start, self.size)]
         part = self.size // 2
@@ -112,6 +112,30 @@
             self.got(sibling_region(shift, k), 9 + {0: 0, 3: 2, 1: 4, 2: 6}[shift] + k)
 
 
+class FarAcross(PartnerFirst):
+    def on_below(self, k):
+        if k == 0:
+            super().on_below(k)
+        else:
+            self.got(self.region(3, k), 1 + k)
+            self.share(3, k)
+
+    def on_above(self, k):
+        if k == 0:
+            super().on_above(k)
+        else:
+            self.got(self.region(1, k), 3 + k)
+            self.share(1, k)
+
+    def on_far(self, k):
+        if k == 0:
+            super().on_far(k)
+            self.put(self.region(2, 0), self.partner, 6)
+        else:
+            self.got(self.region(2, 1), 6)
+            self.share(2, 1)
+
+
 class RingFirst(Copies):
     def share(self, shift, k):
         self.put(self.region(shift, k), self.sibling, 8 + shift * 2 + k)
@@ -190,7 +214,7 @@
 def kernel(
     owner_ref, scale_ref, x_hbm, slot_hbm, gain_ref, w_hbm, wout_hbm, out_ref,
     x_ref, slot_ref, w_ref, tok, ref_tok, wo, kv, query, acc, top, att, att_in, keep, give, moved, arrived,
-    t_send, t_recv, s_send, s_recv, w_send, w_recv, r_send, r_recv, a_send, a_recv,
+    t_send, t_recv, s_send, s_recv, s2_send, s2_recv, w_send, w_recv, r_send, r_recv, a_send, a_recv,
     m_send, m_recv, i_sem,
 ):
     view, seq = lax.axis_index("view"), lax.axis_index("seq")
@@ -230,24 +254,29 @@
         pltpu.make_async_copy(w_hbm.at[j], w_ref.at[:, j * HD : (j + 1) * HD], i_sem.at[3 + j])
         for j in range(3)
     ]
-    for copy in [load_slot, load_x] + load_w + [load_wo]:
+    for copy in [load_slot, load_x, load_wo] + load_w:
         copy.start()
 
-    def seq_place(y_, zh_):
-        return seq_of(y_, zh_, core)
+    def seq_place(stride, base=0):
+        return lambda y_, zh_: seq_of(y_, zh_, core) * stride + base
 
     me = (y, zh)
-    g_t = PartnerFirst(tok, TB, seq_place, me, seq_ring, seq_partner, sibling, t_send, t_recv)
-    g_s = RingFirst(ref_tok, SB, seq_place, me, seq_ring, seq_partner, sibling, s_send, s_recv)
-    g_w = PartnerFirst(wo, TB, seq_place, me, seq_ring, cross, sibling, w_send, w_recv)
+    part = SB // 2
+    g_t = PartnerFirst(tok, TB, seq_place(TB), me, seq_ring, seq_partner, sibling, t_send, t_recv)
+    g_w = FarAcross(wo, TB, seq_place(TB), me, seq_ring, cross, sibling, w_send, w_recv)
+    s_ring = RingFirst(ref_tok, part, seq_place(SB), me, seq_ring, seq_partner, sibling, s_send, s_recv)
+    s_part = PartnerFirst(
+        ref_tok, part, seq_place(SB, part), me, seq_ring, seq_partner, sibling, s2_send, s2_recv
+    )
     g_r = Views(
-        kv, RC, lambda x_, zl_: x_ * 2 + zl_, (x, zl), view_ring, view_partner, None, r_send, r_recv
+        kv, RC, lambda x_, zl_: (x_ * 2 + zl_) * RC, (x, zl), view_ring, view_partner, None, r_send, r_recv
     )
 
-    def of_sibling(buf, size):
+    def of_sibling(buf, size, stride, base=0):
         def region(shift, k):
             zh_ = zh if k == 0 else 1 - zh
-            return buf.at[rows(seq_of(lax.rem(y + shift, 4), zh_, 1 - core) * size, size)]
+            start = seq_of(lax.rem(y + shift, 4), zh_, 1 - core) * stride + base
+            return buf.at[rows(start, size)]
 
         return region
 
@@ -268,7 +297,6 @@
     load_slot.wait()
     give[...] = normalise(slot_ref[rows((1 - zl) * SB, SB), :], gain)
     pl.semaphore_wait(barrier, len(peers))
-    part = SB // 2
     parts = [rows(i * part, part) for i in range(2)]
 
     def swap(i, side):
@@ -326,25 +354,31 @@
         low_part = (scaled - high_part.astype(F32)).astype(BF16)
         query[at, :] = jnp.concatenate([high_part, low_part], axis=1)
 
-    tok_shared = of_sibling(tok, TB)
-    g_s.own()
-    g_t.pass_partner()
+    tok_shared = of_sibling(tok, TB, TB)
+    s_ring.own()
+    s_part.own()
     g_t.on_below(0)
     g_t.on_above(0)
+    s_part.pass_partner()
+    s_ring.on_below()
+    s_ring.on_above()
+    s_part.on_below(0)
+    s_part.on_above(0)
+    s_ring.on_partner(0)
+    s_ring.on_far()
+    s_part.on_below(1)
+    s_part.on_above(1)
+    g_t.pass_partner()
     for copy in load_w:
         copy.wait()
-    g_s.on_below()
-    g_s.on_above()
-    g_s.on_partner(0)
-    g_t.wait_shared(tok_shared, 0)
-    project(y)
-    g_t.on_below(1)
-    g_t.on_above(1)
-    g_s.on_far()
-    g_s.on_partner(1)
-    g_s.on_partner(3)
-    g_s.on_partner(2)
-    g_s.wait_shared(of_sibling(ref_tok, SB))
+    s_ring.on_partner(1)
+    s_ring.on_partner(3)
+    s_part.on_far(0)
+    s_part.on_far(1)
+    s_ring.on_partner(2)
+    s_ring.wait_shared(of_sibling(ref_tok, part, SB))
+    for shift in range(4):
+        s_part.wait_shared(of_sibling(ref_tok, part, SB, part), shift)
 
     def ref_project(i, _):
         own_kv = jnp.dot(ref_tok[rows(i * QB, QB), :], w_ref[:, HD:], preferred_element_type=F32)
@@ -353,44 +387,41 @@
 
     lax.fori_loop(0, RC // QB, ref_project, 0)
     g_r.own()
-    g_t.wait_shared(tok_shared, 3)
-    project(y_down)
-    g_t.wait_shared(tok_shared, 1)
-    project(y_up)
-    g_t.on_far(0)
-    g_t.on_far(1)
-    load_wo.wait()
-    g_w.own()
-    g_t.wait_shared(tok_shared, 2)
-    project(y_far)
-
-    def attend(starts, size, first=False, last=None):
-        count = size * len(starts)
-        pieces = [kv[rows(start, size), :] for start in starts]
-        both = pieces[0] if len(pieces) == 1 else jnp.concatenate(pieces, axis=0)
-        keys = jnp.concatenate([both[:, :HD], both[:, :HD]], axis=1)
-        values = jnp.concatenate([both[:, HD:], jnp.ones((count, HD), BF16)], axis=1)
+
+    begun = set()
+
+    def attend(items, last=None):
+        loaded = {}
 
         def block(t):
             return rows(lax.rem(y + 1 + t, 4) * QB, QB)
 
-        def score(t):
-            return lax.dot_general(query[block(t), :], keys, NT, preferred_element_type=F32)
-
-        ahead = score(0)
-        for t in range(LEN // QB):
+        def score(item):
+            name, start, size, t = item
+            if name not in loaded:
+                both = kv[rows(start, size), :]
+                loaded[name] = (
+                    jnp.concatenate([both[:, :HD], both[:, :HD]], axis=1),
+                    jnp.concatenate([both[:, HD:], jnp.ones((size, HD), BF16)], axis=1),
+                )
+            return lax.dot_general(query[block(t), :], loaded[name][0], NT, preferred_element_type=F32)
+
+        ahead = score(items[0])
+        for index, (name, start, size, t) in enumerate(items):
             scores = ahead
-            if t + 1 < LEN // QB:
-                ahead = score(t + 1)
+            if index + 1 < len(items):
+                ahead = score(items[index + 1])
             q = block(t)
+            first = t not in begun
+            begun.add(t)
             peak = jnp.max(scores, axis=1, keepdims=True)
             if first:
                 new = jnp.broadcast_to(peak, (QB, HD))
             else:
                 old = top[q, :]
                 new = jnp.maximum(old, peak)
-            weights = jnp.exp2(scores - jnp.tile(new, (1, count // HD))).astype(BF16)
-            total = jnp.dot(weights, values, preferred_element_type=F32)
+            weights = jnp.exp2(scores - jnp.tile(new, (1, size // HD))).astype(BF16)
+            total = jnp.dot(weights, loaded[name][1], preferred_element_type=F32)
             if not first:
                 total += acc[q, :] * jnp.tile(jnp.exp2(old - new), (1, 2))
             if last:
@@ -425,31 +456,47 @@
     def group(x_, zl_):
         return (x_ * 2 + zl_) * RC
 
-    attend([4 * LEN], LEN, first=True)
+    def pair(x_, ts=range(4)):
+        return [("pair", group(x_, 0), LEN, t) for t in ts]
+
+    near = (3, 2, 0)
+    g_t.wait_shared(tok_shared, 0)
+    project(y)
+    g_t.on_below(1)
+    g_t.on_above(1)
+    g_t.on_far(0)
+    g_t.wait_shared(tok_shared, 3)
+    project(y_down)
+    g_t.wait_shared(tok_shared, 1)
+    project(y_up)
+    attend([("own", group(x, zl), RC, t) for t in near])
     g_r.on_below()
     g_r.on_above()
     g_r.pass_partner()
-    g_w.pass_partner()
-    attend([group(x, zl)], RC)
+    g_t.on_far(1)
+    load_wo.wait()
+    g_w.own()
+    attend([("partner", group(x, 1 - zl), RC, t) for t in near])
+    g_r.on_far()
+    g_t.wait_shared(tok_shared, 2)
+    project(y_far)
+    attend(pair(x, (1,)) + [("view", 4 * LEN, LEN, t) for t in range(4)])
     g_w.on_below(0)
     g_w.on_above(0)
-    attend([group(x, 1 - zl)], RC)
-    g_r.on_far()
-    attend([group(x_down, zl)], RC)
-    attend([group(x_up, zl)], RC)
+    g_w.pass_partner()
+    g_r.last_below()
+    attend(pair(x_down))
+    g_r.last_above()
+    g_w.on_far(0)
+    attend(pair(x_up))
+    g_r.last_far()
+    attend(pair(x_far), last=hand_out)
+
     g_w.on_below(1)
     g_w.on_above(1)
-    attend([group(x_far, zl)], RC)
-    g_r.last_below()
-    attend([group(x_down, 1 - zl)], RC)
-    g_w.on_far(0)
     g_w.on_far(1)
-    g_r.last_above()
-    g_r.last_far()
-    attend([group(x_up, 1 - zl), group(x_far, 1 - zl)], RC, last=hand_out)
-
     for shift in range(4):
-        g_w.wait_shared(of_sibling(wo, TB), shift)
+        g_w.wait_shared(of_sibling(wo, TB, TB), shift)
     for t in range(4):
         for combo in range(4):
             if t == 3 and combo == 0:
@@ -475,7 +522,7 @@
     for i in range(2):
         swap(i, zl).wait_send()
         move(i, half).wait_send()
-    for gather in (g_t, g_s, g_w, g_r):
+    for gather in (g_t, s_ring, s_part, g_w, g_r):
         gather.close()
     for copy in sent:
         copy.wait_send()
@@ -508,7 +555,7 @@
             pltpu.VMEM((SB, D), BF16),
             pltpu.VMEM((SB, D), BF16),
             pltpu.VMEM((2, SB, D), BF16),
-            dma((17,)), dma((17,)), dma((16,)), dma((16,)), dma((17,)), dma((17,)),
+            dma((17,)), dma((17,)), dma((16,)), dma((16,)), dma((17,)), dma((17,)), dma((17,)), dma((17,)),
             dma((8,)), dma((8,)), dma((16,)), dma((16,)), dma((4,)), dma((6,)), dma((6,)),
         ],
         compiler_params=pltpu.CompilerParams(

time: 120 us -> 115 us (0.958)
  Pallas kernels: 118 us -> 112 us
    pallas_call x1, Pallas kernels: 118 us -> 112 us  [local(): pl.pallas_call(kernel, out_shape=jax.ShapeDtypeStruct((TB, D), BF16), in_...]
where the time goes in v3:
time: 115 us
  Pallas kernels  112 us (97%)
  local copies, waits for them, and re-layouts  1.88 us (2%)
    pallas_call x1, Pallas kernels, local(): pl.pallas_call(kernel, out_shape=jax.ShapeDtypeStruct((TB, D), BF16), in_...  112 us

profile of v3, /device:TPU:1, one launch (start us, length us, event | category | flops | bytes accessed | tf_op | source)
XLA Modules:
  0.0 114.7 jit_solution(9049057057392956016)
XLA Ops:
  0.7 112.2 %shard_map.73 = bf16[128,2048]{1,0:T(8,128)(2,1)} custom-call(s32[4]{0:T(128)} %owner_ref.1, f32[1]{0:T(128)S(6)} %copy.9.scale_ref, bf16[128,2048]{1,0:T(8,128)(2,1)} %bitcast.7, bf16[128,2048]{1,0:T(8,128)(2,1)} %bitcast.8, f32[1,2048]{1,0:T(1,128)} %bitcast.9, bf16[3,2048,128]{2,1,0:T(8,128)(2,1)} %bitcast.6, bf16[128,2048]{1,0:T(8,128)(2,1)} %wout_hbm.1), custom_call_target="tpu_custom_call" | custom-call | flops 17999998976 | bytes 4000000 | tf_op jit(solution)/shard_map/pallas_call | solution.py:536
  112.8 1.9 %copy.10 = bf16[1,128,2048]{2,1,0:T(8,128)(2,1)} copy(bf16[1,128,2048]{2,1,0:T(8,128)(2,1)} %bitcast.5) | data formatting | bytes 1048576

commit v4 on v3

--- a/solution.py
+++ b/solution.py
@@ -296,6 +296,8 @@
     gain = gain_ref[...]
     load_slot.wait()
     give[...] = normalise(slot_ref[rows((1 - zl) * SB, SB), :], gain)
+    load_x.wait()
+    tok[rows(seq * TB, TB), :] = normalise(x_ref[...], gain)
     pl.semaphore_wait(barrier, len(peers))
     parts = [rows(i * part, part) for i in range(2)]
 
@@ -317,8 +319,6 @@
 
     for i in range(2):
         swap(i, zl).start()
-    load_x.wait()
-    tok[rows(seq * TB, TB), :] = normalise(x_ref[...], gain)
     g_t.own()
     keep[zl] = normalise(slot_ref[rows(zl * SB, SB), :], gain)
     for i in range(2):
@@ -483,9 +483,9 @@
     attend(pair(x, (1,)) + [("view", 4 * LEN, LEN, t) for t in range(4)])
     g_w.on_below(0)
     g_w.on_above(0)
-    g_w.pass_partner()
     g_r.last_below()
     attend(pair(x_down))
+    g_w.pass_partner()
     g_r.last_above()
     g_w.on_far(0)
     attend(pair(x_up))

time: 115 us -> 114 us (level)
    pallas_call x1, Pallas kernels: 112 us -> 111 us  [local(): pl.pallas_call(kernel, out_shape=jax.ShapeDtypeStruct((TB, D), BF16), in_...]
where the time goes in v4:
time: 114 us; the launch traced here: 113 us
  Pallas kernels  111 us (97%)
  local copies, waits for them, and re-layouts  1.88 us (2%)
    pallas_call x1, Pallas kernels, local(): pl.pallas_call(kernel, out_shape=jax.ShapeDtypeStruct((TB, D), BF16), in_...  111 us

profile of v4, /device:TPU:1, one launch (start us, length us, event | category | flops | bytes accessed | tf_op | source)
XLA Modules:
  0.0 113.4 jit_solution(2040499396601127102)
XLA Ops:
  0.7 110.8 %shard_map.73 = bf16[128,2048]{1,0:T(8,128)(2,1)} custom-call(s32[4]{0:T(128)} %owner_ref.1, f32[1]{0:T(128)S(6)} %copy.9.scale_ref, bf16[128,2048]{1,0:T(8,128)(2,1)} %bitcast.7, bf16[128,2048]{1,0:T(8,128)(2,1)} %bitcast.8, f32[1,2048]{1,0:T(1,128)} %bitcast.9, bf16[3,2048,128]{2,1,0:T(8,128)(2,1)} %bitcast.6, bf16[128,2048]{1,0:T(8,128)(2,1)} %wout_hbm.1), custom_call_target="tpu_custom_call" | custom-call | flops 17999998976 | bytes 4000000 | tf_op jit(solution)/shard_map/pallas_call | solution.py:536
  111.5 1.9 %copy.10 = bf16[1,128,2048]{2,1,0:T(8,128)(2,1)} copy(bf16[1,128,2048]{2,1,0:T(8,128)(2,1)} %bitcast.5) | data formatting | bytes 1048576

commit v5 on v4

--- a/solution.py
+++ b/solution.py
@@ -80,9 +80,9 @@
 
     def own(self):
         block = self.region(0, 0)
-        self.put(block, self.partner, 0)
         self.put(block, self.ring[0], 1)
         self.put(block, self.ring[1], 3)
+        self.put(block, self.partner, 0)
         self.share(0, 0)
 
     def pass_partner(self):

time: 114 us -> 114 us (level)
  no operation moved by 1% of the time
where the time goes in v5:
time: 114 us; the launch traced here: 113 us
  Pallas kernels  111 us (97%)
  local copies, waits for them, and re-layouts  1.88 us (2%)
    pallas_call x1, Pallas kernels, local(): pl.pallas_call(kernel, out_shape=jax.ShapeDtypeStruct((TB, D), BF16), in_...  111 us

profile of v5, /device:TPU:1, one launch (start us, length us, event | category | flops | bytes accessed | tf_op | source)
XLA Modules:
  0.0 113.4 jit_solution(4781959618742513826)
XLA Ops:
  0.7 110.8 %shard_map.73 = bf16[128,2048]{1,0:T(8,128)(2,1)} custom-call(s32[4]{0:T(128)} %owner_ref.1, f32[1]{0:T(128)S(6)} %copy.9.scale_ref, bf16[128,2048]{1,0:T(8,128)(2,1)} %bitcast.7, bf16[128,2048]{1,0:T(8,128)(2,1)} %bitcast.8, f32[1,2048]{1,0:T(1,128)} %bitcast.9, bf16[3,2048,128]{2,1,0:T(8,128)(2,1)} %bitcast.6, bf16[128,2048]{1,0:T(8,128)(2,1)} %wout_hbm.1), custom_call_target="tpu_custom_call" | custom-call | flops 17999998976 | bytes 4000000 | tf_op jit(solution)/shard_map/pallas_call | solution.py:536
  111.5 1.9 %copy.10 = bf16[1,128,2048]{2,1,0:T(8,128)(2,1)} copy(bf16[1,128,2048]{2,1,0:T(8,128)(2,1)} %bitcast.5) | data formatting | bytes 1048576
